TPU v7x, 128 devices: a whole 4x4x4 slice. The times are simulated.
128 devices in a mesh: dom: 64 (over z, y, x), row: 2 (over core).
Axes of the slice: x: 4, y: 4, z: 4, core: 2. Of those that a mesh axis runs over, the one named last changes fastest.
Arguments:
- right_side: float32 [64, 1024, 512], P('dom', 'row'), may hold values from -6 to 6
- lower_blocks: bfloat16 [64, 6, 1024, 1024], P('dom', None, 'row'), may hold values from -0.15625 to 0.15625
- upper_blocks: bfloat16 [64, 6, 1024, 1024], P('dom', None, 'row'), may hold values from -0.15625 to 0.15625
- final_blocks: bfloat16 [64, 1024, 1024], P('dom', 'row'), may hold values from -0.0234375 to 0.0234375
Outputs:
- solution: float32 [64, 1024, 512], P('dom', 'row')
All inputs are finite; a program needn't handle non-finite values.
Results may differ from a plain program's by a relative error of at most 0.008.
Values may be sent and summed in bfloat16 or wider, within the bound.
A program may use at most 64 MiB of HBM per device.

v0:
```python
import jax
import jax.numpy as jnp
from jax import lax
from jax.sharding import PartitionSpec as P


def shifted(value, axis, steps):
    count = lax.axis_size(axis)
    first, last = (max(0, -steps), min(count, count - steps))
    return lax.ppermute(value, axis, [(source, source + steps) for source in range(first, last)])


def from_everyone(shard, axis):
    count = lax.axis_size(axis)
    return lax.all_to_all(
        jnp.broadcast_to(shard[None], (count, *shard.shape)), axis, 0, 0, tiled=True
    )


def in_order(pieces, dim):
    dims = list(pieces.shape[1:])
    dims[dim] *= pieces.shape[0]
    return jnp.moveaxis(pieces, 0, dim).reshape(dims)


def gathered_copies(shard, axis, dim):
    pieces = from_everyone(shard, axis)
    return in_order(pieces, dim)


def side_by_side(arrays, axis, dim, along):
    both = jnp.concatenate(arrays, axis=along)
    result, at, done = (gathered_copies(both, axis, dim), 0, [])
    for a in arrays:
        done.append(lax.slice_in_dim(result, at, at + a.shape[along], axis=along))
        at += a.shape[along]
    return tuple(done)


def body(right_side, lower_blocks, upper_blocks, final_blocks):
    current = right_side[0]
    levels = lower_blocks.shape[1]
    for level_index in range(levels):
        distance = 2**level_index
        rounded = current.astype(jnp.bfloat16)
        from_low = shifted(rounded, "dom", distance)
        from_high = shifted(rounded, "dom", -distance)
        full_low, full_high = side_by_side((from_low, from_high), "row", 0, 1)
        current = (
            current
            + jnp.dot(lower_blocks[0, level_index], full_low, preferred_element_type=jnp.float32)
            + jnp.dot(upper_blocks[0, level_index], full_high, preferred_element_type=jnp.float32)
        )
    gathered = gathered_copies(current.astype(jnp.bfloat16), "row", 0)
    solution = jnp.dot(final_blocks[0], gathered, preferred_element_type=jnp.float32)
    return solution[None]


def solution(mesh):
    in_specs = (
        P("dom", "row", None),
        P("dom", None, "row", None),
        P("dom", None, "row", None),
        P("dom", "row", None),
    )
    out_specs = P("dom", "row", None)
    return jax.shard_map(body, mesh=mesh, in_specs=in_specs, out_specs=out_specs, check_vma=False)
```

profile of v0, /device:TPU:5, one launch (start us, length us, event | category | flops | bytes accessed | tf_op | source)
XLA Modules:
  0.0 214.6 jit_solution(6337286685741733062)
XLA Ops:
  3.9 3.1 %collective-permute-start = (bf16[512,512]{0,1:T(8,128)(2,1)S(1)}, bf16[512,512]{0,1:T(8,128)(2,1)S(1)}, u32[]{:S(2)}, u32[]{:S(2)}) collective-permute-start(bf16[512,512]{0,1:T(8,128)(2,1)S(1)} %bitcast_convert_fusion), channel_id=1, source_target_pairs={{0,2},{2,4},{4,6},{6,8},{8,10},{10,12},{12,14},{14,16},{16,18},{18... | collective-permute-start | bytes 1572872 | tf_op jit(solution)/shard_map/ppermute | solution.py:10
  7.0 9.4 %collective-permute-done.1 = bf16[512,512]{0,1:T(8,128)(2,1)S(1)} collective-permute-done((bf16[512,512]{0,1:T(8,128)(2,1)S(1)}, bf16[512,512]{0,1:T(8,128)(2,1)S(1)}, u32[]{:S(2)}, u32[]{:S(2)}) %collective-permute-start.1) | collective-permute-done | bytes 524320 | tf_op jit(solution)/shard_map/ppermute | solution.py:10
  21.1 6.9 %all_to_all.35 = bf16[2,512,1024]{2,1,0:T(8,128)(2,1)S(1)} all-to-all(bf16[2,512,1024]{2,1,0:T(8,128)(2,1)S(1)} %broadcast_in_dim.16), channel_id=1, replica_groups=mesh['dom'=64,'row'=2] {'row'}, dimensions={0} | all-to-all | bytes 4194304 | tf_op jit(solution)/shard_map/all_to_all | solution.py:15
  34.8 7.4 %collective-permute-start.2 = (bf16[512,512]{0,1:T(8,128)(2,1)S(1)}, bf16[512,512]{0,1:T(8,128)(2,1)S(1)}, u32[]{:S(2)}, u32[]{:S(2)}) collective-permute-start(bf16[512,512]{0,1:T(8,128)(2,1)S(1)} %get-tuple-element.5), channel_id=1, source_target_pairs={{0,4},{2,6},{4,8},{6,10},{8,12},{10,14},{12,16},{14,18},{16,20},{1... | collective-permute-start | bytes 1572872 | tf_op jit(solution)/shard_map/ppermute | solution.py:10
  42.2 10.0 %collective-permute-done.3 = bf16[512,512]{0,1:T(8,128)(2,1)S(1)} collective-permute-done((bf16[512,512]{0,1:T(8,128)(2,1)S(1)}, bf16[512,512]{0,1:T(8,128)(2,1)S(1)}, u32[]{:S(2)}, u32[]{:S(2)}) %collective-permute-start.3) | collective-permute-done | bytes 524320 | tf_op jit(solution)/shard_map/ppermute | solution.py:10
  52.3 5.0 %collective-permute-done.2 = bf16[512,512]{0,1:T(8,128)(2,1)S(1)} collective-permute-done((bf16[512,512]{0,1:T(8,128)(2,1)S(1)}, bf16[512,512]{0,1:T(8,128)(2,1)S(1)}, u32[]{:S(2)}, u32[]{:S(2)}) %collective-permute-start.2) | collective-permute-done | bytes 524320 | tf_op jit(solution)/shard_map/ppermute | solution.py:10
  58.2 6.1 %all_to_all.36 = bf16[2,512,1024]{2,1,0:T(8,128)(2,1)S(1)} all-to-all(bf16[2,512,1024]{2,1,0:T(8,128)(2,1)S(1)} %broadcast_in_dim.17), channel_id=1, replica_groups=mesh['dom'=64,'row'=2] {'row'}, dimensions={0} | all-to-all | bytes 4194304 | tf_op jit(solution)/shard_map/all_to_all | solution.py:15
  66.3 3.0 %fusion.51 = (bf16[512,512]{0,1:T(8,128)(2,1)S(1)}, f32[512,512]{0,1:T(8,128)}) fusion(f32[512,512]{0,1:T(8,128)S(1)} %fusion.9, bf16[1,6,512,1024]{3,2,1,0:T(8,128)(2,1)} %param.6, bf16[1024,1024]{1,0:T(8,128)(2,1)S(1)} %bitcast.115), kind=kOutput, calls=%fused_computation.71 | convolution fusion | flops 537395200 | bytes 4718592 | tf_op jit(solution)/shard_map/dot_general | solution.py:52
  70.5 9.0 %collective-permute-start.4 = (bf16[512,512]{0,1:T(8,128)(2,1)S(1)}, bf16[512,512]{0,1:T(8,128)(2,1)S(1)}, u32[]{:S(2)}, u32[]{:S(2)}) collective-permute-start(bf16[512,512]{0,1:T(8,128)(2,1)S(1)} %get-tuple-element.7), channel_id=1, source_target_pairs={{0,8},{2,10},{4,12},{6,14},{8,16},{10,18},{12,20},{14,22},{16,24},... | collective-permute-start | bytes 1572872 | tf_op jit(solution)/shard_map/ppermute | solution.py:10
  79.6 10.0 %collective-permute-done.5 = bf16[512,512]{0,1:T(8,128)(2,1)S(1)} collective-permute-done((bf16[512,512]{0,1:T(8,128)(2,1)S(1)}, bf16[512,512]{0,1:T(8,128)(2,1)S(1)}, u32[]{:S(2)}, u32[]{:S(2)}) %collective-permute-start.5) | collective-permute-done | bytes 524320 | tf_op jit(solution)/shard_map/ppermute | solution.py:10
  91.3 6.4 %all_to_all.37 = bf16[2,512,1024]{2,1,0:T(8,128)(2,1)S(1)} all-to-all(bf16[2,512,1024]{2,1,0:T(8,128)(2,1)S(1)} %broadcast_in_dim.18), channel_id=1, replica_groups=mesh['dom'=64,'row'=2] {'row'}, dimensions={0} | all-to-all | bytes 4194304 | tf_op jit(solution)/shard_map/all_to_all | solution.py:15
  99.7 3.0 %fusion.52 = (bf16[512,512]{0,1:T(8,128)(2,1)S(1)}, f32[512,512]{0,1:T(8,128)}) fusion(f32[512,512]{0,1:T(8,128)S(1)} %fusion.7, bf16[1,6,512,1024]{3,2,1,0:T(8,128)(2,1)} %param.6, bf16[1024,1024]{1,0:T(8,128)(2,1)S(1)} %bitcast.117), kind=kOutput, calls=%fused_computation.72 | convolution fusion | flops 537395200 | bytes 4718592 | tf_op jit(solution)/shard_map/dot_general | solution.py:52
  104.0 6.5 %collective-permute-start.6 = (bf16[512,512]{0,1:T(8,128)(2,1)S(1)}, bf16[512,512]{0,1:T(8,128)(2,1)S(1)}, u32[]{:S(2)}, u32[]{:S(2)}) collective-permute-start(bf16[512,512]{0,1:T(8,128)(2,1)S(1)} %get-tuple-element.9), channel_id=1, source_target_pairs={{0,16},{2,18},{4,20},{6,22},{8,24},{10,26},{12,28},{14,30},{16,32}... | collective-permute-start | bytes 1572872 | tf_op jit(solution)/shard_map/ppermute | solution.py:10
  110.5 10.0 %collective-permute-done.7 = bf16[512,512]{0,1:T(8,128)(2,1)S(1)} collective-permute-done((bf16[512,512]{0,1:T(8,128)(2,1)S(1)}, bf16[512,512]{0,1:T(8,128)(2,1)S(1)}, u32[]{:S(2)}, u32[]{:S(2)}) %collective-permute-start.7) | collective-permute-done | bytes 524320 | tf_op jit(solution)/shard_map/ppermute | solution.py:10
  122.3 6.4 %all_to_all.38 = bf16[2,512,1024]{2,1,0:T(8,128)(2,1)S(1)} all-to-all(bf16[2,512,1024]{2,1,0:T(8,128)(2,1)S(1)} %broadcast_in_dim.19), channel_id=1, replica_groups=mesh['dom'=64,'row'=2] {'row'}, dimensions={0} | all-to-all | bytes 4194304 | tf_op jit(solution)/shard_map/all_to_all | solution.py:15
  130.7 3.0 %fusion.53 = (bf16[512,512]{0,1:T(8,128)(2,1)S(1)}, f32[512,512]{0,1:T(8,128)}) fusion(f32[512,512]{0,1:T(8,128)S(1)} %fusion.5, bf16[1,6,512,1024]{3,2,1,0:T(8,128)(2,1)} %param.6, bf16[1024,1024]{1,0:T(8,128)(2,1)S(1)} %bitcast.119), kind=kOutput, calls=%fused_computation.73 | convolution fusion | flops 537395200 | bytes 4718592 | tf_op jit(solution)/shard_map/dot_general | solution.py:52
  134.9 16.8 %collective-permute-start.8 = (bf16[512,512]{0,1:T(8,128)(2,1)S(1)}, bf16[512,512]{0,1:T(8,128)(2,1)S(1)}, u32[]{:S(2)}, u32[]{:S(2)}) collective-permute-start(bf16[512,512]{0,1:T(8,128)(2,1)S(1)} %get-tuple-element.11), channel_id=1, source_target_pairs={{0,32},{2,34},{4,36},{6,38},{8,40},{10,42},{12,44},{14,46},{16,48}... | collective-permute-start | bytes 1572872 | tf_op jit(solution)/shard_map/ppermute | solution.py:10
  151.7 10.0 %collective-permute-done.9 = bf16[512,512]{0,1:T(8,128)(2,1)S(1)} collective-permute-done((bf16[512,512]{0,1:T(8,128)(2,1)S(1)}, bf16[512,512]{0,1:T(8,128)(2,1)S(1)}, u32[]{:S(2)}, u32[]{:S(2)}) %collective-permute-start.9) | collective-permute-done | bytes 524320 | tf_op jit(solution)/shard_map/ppermute | solution.py:10
  163.5 6.4 %all_to_all.39 = bf16[2,512,1024]{2,1,0:T(8,128)(2,1)S(1)} all-to-all(bf16[2,512,1024]{2,1,0:T(8,128)(2,1)S(1)} %broadcast_in_dim.20), channel_id=1, replica_groups=mesh['dom'=64,'row'=2] {'row'}, dimensions={0} | all-to-all | bytes 4194304 | tf_op jit(solution)/shard_map/all_to_all | solution.py:15
  171.9 3.0 %fusion.54 = (bf16[512,512]{0,1:T(8,128)(2,1)S(1)}, f32[512,512]{0,1:T(8,128)}) fusion(f32[512,512]{0,1:T(8,128)S(1)} %fusion.3, bf16[1,6,512,1024]{3,2,1,0:T(8,128)(2,1)} %param.6, bf16[1024,1024]{1,0:T(8,128)(2,1)S(1)} %bitcast.121), kind=kOutput, calls=%fused_computation.74 | convolution fusion | flops 537395200 | bytes 4718592 | tf_op jit(solution)/shard_map/dot_general | solution.py:52
  176.2 9.4 %collective-permute-start.10 = (bf16[512,512]{0,1:T(8,128)(2,1)S(1)}, bf16[512,512]{0,1:T(8,128)(2,1)S(1)}, u32[]{:S(2)}, u32[]{:S(2)}) collective-permute-start(bf16[512,512]{0,1:T(8,128)(2,1)S(1)} %get-tuple-element.13), channel_id=1, source_target_pairs={{0,64},{2,66},{4,68},{6,70},{8,72},{10,74},{12,76},{14,78},{16,80}... | collective-permute-start | bytes 1572872 | tf_op jit(solution)/shard_map/ppermute | solution.py:10
  185.5 10.1 %collective-permute-done.11 = bf16[512,512]{0,1:T(8,128)(2,1)S(1)} collective-permute-done((bf16[512,512]{0,1:T(8,128)(2,1)S(1)}, bf16[512,512]{0,1:T(8,128)(2,1)S(1)}, u32[]{:S(2)}, u32[]{:S(2)}) %collective-permute-start.11) | collective-permute-done | bytes 524320 | tf_op jit(solution)/shard_map/ppermute | solution.py:10
  197.4 6.3 %all_to_all.40 = bf16[2,512,1024]{2,1,0:T(8,128)(2,1)S(1)} all-to-all(bf16[2,512,1024]{2,1,0:T(8,128)(2,1)S(1)} %broadcast_in_dim.21), channel_id=1, replica_groups=mesh['dom'=64,'row'=2] {'row'}, dimensions={0} | all-to-all | bytes 4194304 | tf_op jit(solution)/shard_map/all_to_all | solution.py:15
  208.0 4.6 %all_to_all.41 = bf16[2,512,512]{2,1,0:T(8,128)(2,1)S(1)} all-to-all(bf16[2,512,512]{2,1,0:T(8,128)(2,1)S(1)} %broadcast_in_dim.22), channel_id=1, replica_groups=mesh['dom'=64,'row'=2] {'row'}, dimensions={0} | all-to-all | bytes 2097152 | tf_op jit(solution)/shard_map/all_to_all | solution.py:15
  (55 shorter events, 42.5 us)
Async XLA Ops:
  0.0 212.6 %copy-start = (bf16[1,512,1024]{2,1,0:T(8,128)(2,1)S(1)}, bf16[1,512,1024]{2,1,0:T(8,128)(2,1)}, u32[]{:S(2)}) copy-start(bf16[1,512,1024]{2,1,0:T(8,128)(2,1)} %param.7) | copy-start | bytes 3145732
  1.7 14.7 %collective-permute-start.1 = (bf16[512,512]{0,1:T(8,128)(2,1)S(1)}, bf16[512,512]{0,1:T(8,128)(2,1)S(1)}, u32[]{:S(2)}, u32[]{:S(2)}) collective-permute-start(bf16[512,512]{0,1:T(8,128)(2,1)S(1)} %bitcast_convert_fusion), channel_id=1, source_target_pairs={{2,0},{4,2},{6,4},{8,6},{10,8},{12,10},{14,12},{16,14},{18,16},{20... | collective-permute-start | bytes 1572872 | tf_op jit(solution)/shard_map/ppermute | solution.py:10
  3.9 14.4 %collective-permute-start = (bf16[512,512]{0,1:T(8,128)(2,1)S(1)}, bf16[512,512]{0,1:T(8,128)(2,1)S(1)}, u32[]{:S(2)}, u32[]{:S(2)}) collective-permute-start(bf16[512,512]{0,1:T(8,128)(2,1)S(1)} %bitcast_convert_fusion), channel_id=1, source_target_pairs={{0,2},{2,4},{4,6},{6,8},{8,10},{10,12},{12,14},{14,16},{16,18},{18... | collective-permute-start | bytes 1572872 | tf_op jit(solution)/shard_map/ppermute | solution.py:10
  32.9 19.3 %collective-permute-start.3 = (bf16[512,512]{0,1:T(8,128)(2,1)S(1)}, bf16[512,512]{0,1:T(8,128)(2,1)S(1)}, u32[]{:S(2)}, u32[]{:S(2)}) collective-permute-start(bf16[512,512]{0,1:T(8,128)(2,1)S(1)} %get-tuple-element.5), channel_id=1, source_target_pairs={{4,0},{6,2},{8,4},{10,6},{12,8},{14,10},{16,12},{18,14},{20,16},{2... | collective-permute-start | bytes 1572872 | tf_op jit(solution)/shard_map/ppermute | solution.py:10
  34.8 22.5 %collective-permute-start.2 = (bf16[512,512]{0,1:T(8,128)(2,1)S(1)}, bf16[512,512]{0,1:T(8,128)(2,1)S(1)}, u32[]{:S(2)}, u32[]{:S(2)}) collective-permute-start(bf16[512,512]{0,1:T(8,128)(2,1)S(1)} %get-tuple-element.5), channel_id=1, source_target_pairs={{0,4},{2,6},{4,8},{6,10},{8,12},{10,14},{12,16},{14,18},{16,20},{1... | collective-permute-start | bytes 1572872 | tf_op jit(solution)/shard_map/ppermute | solution.py:10
  58.2 6.1 %copy-start.1 = (f32[512,512]{0,1:T(8,128)S(1)}, f32[512,512]{0,1:T(8,128)}, u32[]{:S(2)}) copy-start(f32[512,512]{0,1:T(8,128)} %get-tuple-element.6) | copy-start | bytes 3145732
  69.2 20.4 %collective-permute-start.5 = (bf16[512,512]{0,1:T(8,128)(2,1)S(1)}, bf16[512,512]{0,1:T(8,128)(2,1)S(1)}, u32[]{:S(2)}, u32[]{:S(2)}) collective-permute-start(bf16[512,512]{0,1:T(8,128)(2,1)S(1)} %get-tuple-element.7), channel_id=1, source_target_pairs={{8,0},{10,2},{12,4},{14,6},{16,8},{18,10},{20,12},{22,14},{24,16},... | collective-permute-start | bytes 1572872 | tf_op jit(solution)/shard_map/ppermute | solution.py:10
  70.5 19.9 %collective-permute-start.4 = (bf16[512,512]{0,1:T(8,128)(2,1)S(1)}, bf16[512,512]{0,1:T(8,128)(2,1)S(1)}, u32[]{:S(2)}, u32[]{:S(2)}) collective-permute-start(bf16[512,512]{0,1:T(8,128)(2,1)S(1)} %get-tuple-element.7), channel_id=1, source_target_pairs={{0,8},{2,10},{4,12},{6,14},{8,16},{10,18},{12,20},{14,22},{16,24},... | collective-permute-start | bytes 1572872 | tf_op jit(solution)/shard_map/ppermute | solution.py:10
  91.3 6.4 %copy-start.2 = (f32[512,512]{0,1:T(8,128)S(1)}, f32[512,512]{0,1:T(8,128)}, u32[]{:S(2)}) copy-start(f32[512,512]{0,1:T(8,128)} %get-tuple-element.8) | copy-start | bytes 3145732
  102.7 17.9 %collective-permute-start.7 = (bf16[512,512]{0,1:T(8,128)(2,1)S(1)}, bf16[512,512]{0,1:T(8,128)(2,1)S(1)}, u32[]{:S(2)}, u32[]{:S(2)}) collective-permute-start(bf16[512,512]{0,1:T(8,128)(2,1)S(1)} %get-tuple-element.9), channel_id=1, source_target_pairs={{16,0},{18,2},{20,4},{22,6},{24,8},{26,10},{28,12},{30,14},{32,16}... | collective-permute-start | bytes 1572872 | tf_op jit(solution)/shard_map/ppermute | solution.py:10
  104.0 17.4 %collective-permute-start.6 = (bf16[512,512]{0,1:T(8,128)(2,1)S(1)}, bf16[512,512]{0,1:T(8,128)(2,1)S(1)}, u32[]{:S(2)}, u32[]{:S(2)}) collective-permute-start(bf16[512,512]{0,1:T(8,128)(2,1)S(1)} %get-tuple-element.9), channel_id=1, source_target_pairs={{0,16},{2,18},{4,20},{6,22},{8,24},{10,26},{12,28},{14,30},{16,32}... | collective-permute-start | bytes 1572872 | tf_op jit(solution)/shard_map/ppermute | solution.py:10
  122.3 6.4 %copy-start.3 = (f32[512,512]{0,1:T(8,128)S(1)}, f32[512,512]{0,1:T(8,128)}, u32[]{:S(2)}) copy-start(f32[512,512]{0,1:T(8,128)} %get-tuple-element.10) | copy-start | bytes 3145732
  133.6 28.1 %collective-permute-start.9 = (bf16[512,512]{0,1:T(8,128)(2,1)S(1)}, bf16[512,512]{0,1:T(8,128)(2,1)S(1)}, u32[]{:S(2)}, u32[]{:S(2)}) collective-permute-start(bf16[512,512]{0,1:T(8,128)(2,1)S(1)} %get-tuple-element.11), channel_id=1, source_target_pairs={{32,0},{34,2},{36,4},{38,6},{40,8},{42,10},{44,12},{46,14},{48,16}... | collective-permute-start | bytes 1572872 | tf_op jit(solution)/shard_map/ppermute | solution.py:10
  134.9 27.7 %collective-permute-start.8 = (bf16[512,512]{0,1:T(8,128)(2,1)S(1)}, bf16[512,512]{0,1:T(8,128)(2,1)S(1)}, u32[]{:S(2)}, u32[]{:S(2)}) collective-permute-start(bf16[512,512]{0,1:T(8,128)(2,1)S(1)} %get-tuple-element.11), channel_id=1, source_target_pairs={{0,32},{2,34},{4,36},{6,38},{8,40},{10,42},{12,44},{14,46},{16,48}... | collective-permute-start | bytes 1572872 | tf_op jit(solution)/shard_map/ppermute | solution.py:10
  163.5 6.4 %copy-start.4 = (f32[512,512]{0,1:T(8,128)S(1)}, f32[512,512]{0,1:T(8,128)}, u32[]{:S(2)}) copy-start(f32[512,512]{0,1:T(8,128)} %get-tuple-element.12) | copy-start | bytes 3145732
  174.9 20.7 %collective-permute-start.11 = (bf16[512,512]{0,1:T(8,128)(2,1)S(1)}, bf16[512,512]{0,1:T(8,128)(2,1)S(1)}, u32[]{:S(2)}, u32[]{:S(2)}) collective-permute-start(bf16[512,512]{0,1:T(8,128)(2,1)S(1)} %get-tuple-element.13), channel_id=1, source_target_pairs={{64,0},{66,2},{68,4},{70,6},{72,8},{74,10},{76,12},{78,14},{80,16}... | collective-permute-start | bytes 1572872 | tf_op jit(solution)/shard_map/ppermute | solution.py:10
  176.2 20.3 %collective-permute-start.10 = (bf16[512,512]{0,1:T(8,128)(2,1)S(1)}, bf16[512,512]{0,1:T(8,128)(2,1)S(1)}, u32[]{:S(2)}, u32[]{:S(2)}) collective-permute-start(bf16[512,512]{0,1:T(8,128)(2,1)S(1)} %get-tuple-element.13), channel_id=1, source_target_pairs={{0,64},{2,66},{4,68},{6,70},{8,72},{10,74},{12,76},{14,78},{16,80}... | collective-permute-start | bytes 1572872 | tf_op jit(solution)/shard_map/ppermute | solution.py:10
  197.4 6.3 %copy-start.5 = (f32[512,512]{0,1:T(8,128)S(1)}, f32[512,512]{0,1:T(8,128)}, u32[]{:S(2)}) copy-start(f32[512,512]{0,1:T(8,128)} %get-tuple-element.14) | copy-start | bytes 3145732
where the time goes:
time: 218 us; the launch traced here: 215 us
  waiting for transfers between devices  69.9 us (32%)
  starting transfers between devices  61.4 us (28%)
  blocking collectives  43 us (20%)
  matrix products  29.5 us (14%)
  local copies, waits for them, and re-layouts  8.93 us (4%)
    ppermute x12, waiting for transfers between devices, shifted(): lax.ppermute(value, axis, [(source, source + steps) for source in range(f...  69.9 us
    ppermute x12, starting transfers between devices, shifted(): lax.ppermute(value, axis, [(source, source + steps) for source in range(f...  61.4 us
    all_to_all x7, blocking collectives, from_everyone(): lax.all_to_all(jnp.broadcast_to(shard[None], (count, *shard.shape)), axis...  43 us
    dot_general x6, matrix products, body(): jnp.dot(upper_blocks[0, level_index], full_high, preferred_element_type=j...  16.8 us
    dot_general x6, matrix products, body(): jnp.dot(lower_blocks[0, level_index], full_low, preferred_element_type=jn...  11.9 us
  transfers between devices with their start and end apart: 12, of which 12 were waited for; matrix products, arithmetic and copies ran while one was open for 0% of the time, Pallas kernels for 0%

commit v1 on v0

v1 whole, which is shorter than its diff:
```python
import functools

import jax
import jax.numpy as jnp
from jax import lax
from jax.experimental import pallas as pl
from jax.experimental.pallas import tpu as pltpu
from jax.sharding import PartitionSpec as P

MESH = pl.DeviceIdType.MESH
CHUNKS = 4
LAG = 1
EARLY = True


def kernel(slices, levels, rs_ref, lo_ref, up_ref, fin_ref, out_ref,
           lo_v, up_v, fin_v, cur, snd, low, high, gat,
           load_sem, s_sem, r_sem, fs_sem, fr_sem, gs_sem, gr_sem):
    half, cols = snd.shape[2], snd.shape[3]
    chunks = snd.shape[1]
    me, row = lax.axis_index("dom"), lax.axis_index("row")
    sib = 1 - row
    mine = pl.ds(pl.multiple_of(row * half, half), half)

    loads = []
    for l in range(levels):
        loads.append((
            pltpu.make_async_copy(lo_ref.at[0, l], lo_v.at[l], load_sem.at[0, l]),
            pltpu.make_async_copy(up_ref.at[0, l], up_v.at[l], load_sem.at[1, l])))
    loads.append((pltpu.make_async_copy(fin_ref.at[0], fin_v, load_sem.at[0, levels]),))
    for group in loads:
        for copy in group:
            copy.start()

    barrier = pltpu.get_barrier_semaphore()
    pl.semaphore_signal(barrier, inc=1, device_id=(me, sib), device_id_type=MESH)
    count = 1
    for l in range(levels):
        d = 2 ** l
        for ok, peer in ((me >= d, me - d), (me + d < slices, me + d)):
            count = count + ok.astype(jnp.int32)

            @pl.when(ok)
            def _():
                pl.semaphore_signal(barrier, inc=1, device_id=(peer, row), device_id_type=MESH)
    pl.semaphore_wait(barrier, count)

    def sides(l):
        d = 2 ** l
        return ((me + d < slices, me + d, me >= d, low), (me >= d, me - d, me + d < slices, high))

    def send(c, l, side, peer, buf):
        return pltpu.make_async_remote_copy(
            snd.at[l, c], buf.at[l, c, mine], s_sem.at[side, l, c], r_sem.at[side, l, c], (peer, row), MESH)

    def forward(c, l, side, buf):
        return pltpu.make_async_remote_copy(
            buf.at[l, c, mine], buf.at[l, c, mine], fs_sem.at[side, l, c], fr_sem.at[side, l, c], (me, sib), MESH)

    def share(c):
        return pltpu.make_async_remote_copy(
            gat.at[c, mine], gat.at[c, mine], gs_sem.at[c], gr_sem.at[c], (me, sib), MESH)

    def do_send(c, l):
        lanes = slice(c * cols, (c + 1) * cols)
        source = rs_ref[0, :, lanes] if l == 0 else cur[:, lanes]
        if l == levels:
            gat[c, mine] = source.astype(jnp.bfloat16)
            share(c).start()
            return
        snd[l, c] = source.astype(jnp.bfloat16)
        for side, (to, peer, _, buf) in enumerate(sides(l)):
            @pl.when(to)
            def _():
                send(c, l, side, peer, buf).start()

    def do_forward(c, l):
        if l == levels:
            return
        for side, (_, peer, got, buf) in enumerate(sides(l)):
            @pl.when(got)
            def _():
                send(c, l, side, peer, buf).wait_recv()
                forward(c, l, side, buf).start()

    def do_math(c, l):
        lanes = slice(c * cols, (c + 1) * cols)
        if l == levels:
            share(c).wait_recv()
            if c == 0:
                loads[l][0].wait()
            out_ref[0, :, lanes] = jnp.dot(fin_v[...], gat[c], preferred_element_type=jnp.float32)
            return
        if c == 0:
            for copy in loads[l]:
                copy.wait()
        if l == 0:
            cur[:, lanes] = rs_ref[0, :, lanes]
        for side, (_, _, got, buf) in enumerate(sides(l)):
            weights = (lo_v, up_v)[side]

            @pl.when(got)
            def _():
                forward(c, l, side, buf).wait_recv()
                cur[:, lanes] += jnp.dot(weights[l], buf[l, c], preferred_element_type=jnp.float32)

    if EARLY:
        for c in range(chunks):
            do_send(c, 0)
    for step in range(levels + 1 + LAG * (chunks - 1)):
        active = [(c, step - LAG * c) for c in range(chunks) if 0 <= step - LAG * c <= levels]
        if not EARLY:
            for c, l in active:
                if l == 0:
                    do_send(c, 0)
        for c, l in active:
            do_forward(c, l)
        for c, l in active:
            do_math(c, l)
            if l < levels:
                do_send(c, l + 1)

    for c in range(chunks):
        for l in range(levels):
            for side, (to, peer, got, buf) in enumerate(sides(l)):
                @pl.when(to)
                def _():
                    send(c, l, side, peer, buf).wait_send()

                @pl.when(got)
                def _():
                    forward(c, l, side, buf).wait_send()
        share(c).wait_send()


def solution(mesh):
    slices = mesh.shape["dom"]

    def body(right_side, lower_blocks, upper_blocks, final_blocks):
        _, levels, half, width = lower_blocks.shape
        rhs = right_side.shape[2]
        chunks = CHUNKS
        cols = rhs // chunks
        bf = jnp.bfloat16
        any_, vm = pl.BlockSpec(memory_space=pl.ANY), pl.BlockSpec(memory_space=pltpu.VMEM)
        dma = pltpu.SemaphoreType.DMA
        return pl.pallas_call(
            functools.partial(kernel, slices, levels),
            out_shape=jax.ShapeDtypeStruct(right_side.shape, jnp.float32),
            in_specs=[vm, any_, any_, any_],
            out_specs=vm,
            scratch_shapes=[
                pltpu.VMEM((levels, half, width), bf),
                pltpu.VMEM((levels, half, width), bf),
                pltpu.VMEM((half, width), bf),
                pltpu.VMEM((half, rhs), jnp.float32),
                pltpu.VMEM((levels, chunks, half, cols), bf),
                pltpu.VMEM((levels, chunks, width, cols), bf),
                pltpu.VMEM((levels, chunks, width, cols), bf),
                pltpu.VMEM((chunks, width, cols), bf),
                dma((2, levels + 1)),
                dma((2, levels, chunks)),
                dma((2, levels, chunks)),
                dma((2, levels, chunks)),
                dma((2, levels, chunks)),
                dma((chunks,)),
                dma((chunks,)),
            ],
            compiler_params=pltpu.CompilerParams(
                collective_id=0, has_side_effects=True, vmem_limit_bytes=56 * 2**20),
        )(right_side, lower_blocks, upper_blocks, final_blocks)

    in_specs = (
        P("dom", "row", None),
        P("dom", None, "row", None),
        P("dom", None, "row", None),
        P("dom", "row", None),
    )
    return jax.shard_map(body, mesh=mesh, in_specs=in_specs, out_specs=P("dom", "row", None), check_vma=False)
```

time: 218 us -> 119 us (0.55)
  Pallas kernels: 0 us -> 115 us
  waiting for transfers between devices: 69.9 us -> 0 us
  starting transfers between devices: 61.4 us -> 0 us
  blocking collectives: 43 us -> 0 us
  matrix products: 29.5 us -> 0 us
  local copies, waits for them, and re-layouts: 8.93 us -> 2.26 us
    pallas_call x0 -> x1, Pallas kernels: none -> 115 us  [body(): pl.pallas_call(functools.partial(kernel, slices, levels), out_shape=jax.S...]
    ppermute x12 -> x0, waiting for transfers between devices: 69.9 us -> none  [shifted(): lax.ppermute(value, axis, [(source, source + steps) for source in range(f...]
    ppermute x12 -> x0, starting transfers between devices: 61.4 us -> none  [shifted(): lax.ppermute(value, axis, [(source, source + steps) for source in range(f...]
    all_to_all x7 -> x0, blocking collectives: 43 us -> none  [from_everyone(): lax.all_to_all(jnp.broadcast_to(shard[None], (count, *shard.shape)), axis...]
    dot_general x13 -> x0, matrix products: 29.5 us -> none  [the longest x6 16.8 us: body(): jnp.dot(upper_blocks[0, level_index], full_high, preferred_element_type=j...]
    concatenate x6 -> x0, local copies, waits for them, and re-layouts: 4.16 us -> none  [side_by_side(): both = jnp.concatenate(arrays, axis=along)]
    broadcast_in_dim x8 -> x0, local copies, waits for them, and re-layouts: 2.88 us -> none  [the longest x7 1.57 us: from_everyone(): jnp.broadcast_to(shard[None], (count, *shard.shape))]
  transfers between devices with their start and end apart: 12 -> 0, of which waited for: 12 -> 0; matrix products, arithmetic and copies ran while one was open for 0% -> 0% of each run, Pallas kernels for 0% -> 0%
where the time goes in v1:
time: 119 us; the launch traced here: 118 us
  Pallas kernels  115 us (97%)
  local copies, waits for them, and re-layouts  2.26 us (2%)
    pallas_call x1, Pallas kernels, body(): pl.pallas_call(functools.partial(kernel, slices, levels), out_shape=jax.S...  115 us

profile of v1, /device:TPU:5, one launch (start us, length us, event | category | flops | bytes accessed | tf_op | source)
XLA Modules:
  0.0 117.6 jit_solution(1624710529203139743)
XLA Ops:
  0.0 115.3 %shard_map.46 = f32[1,512,512]{2,1,0:T(8,128)} custom-call(f32[1,512,512]{2,1,0:T(8,128)} %rs_ref.1, bf16[1,6,512,1024]{3,2,1,0:T(8,128)(2,1)} %lo_ref.1, bf16[1,6,512,1024]{3,2,1,0:T(8,128)(2,1)} %up_ref.1, bf16[1,512,1024]{2,1,0:T(8,128)(2,1)} %fin_ref.1), custom_call_target="tpu_custom_call" | custom-call | tf_op jit(solution)/shard_map/pallas_call | solution.py:147
  115.3 2.3 %copy.6 = f32[1,512,512]{2,1,0:T(8,128)} copy(f32[1,512,512]{2,1,0:T(8,128)} %shard_map.46) | data formatting | bytes 2097152

commit v2 on v0

v2 whole, which is shorter than its diff:
```python
import functools

import jax
import jax.numpy as jnp
from jax import lax
from jax.experimental import pallas as pl
from jax.experimental.pallas import tpu as pltpu
from jax.sharding import PartitionSpec as P

MESH = pl.DeviceIdType.MESH
LANES = 128
BLOCK = 256
AHEAD = 2
GATE = (0, 0)


def schedule(chunks, levels):
    return [(step - c, c) for step in range(levels + chunks) for c in range(chunks) if 0 <= step - c <= levels]


def kernel(slices, levels, rs_ref, lo_ref, up_ref, state_ref,
           lo_v, up_v, cur, first, snd, low, high,
           w_sem, w_send, w_recv, x_sem, x_send, x_recv,
           f_send, f_recv, s_sem, r_sem, l_sem, o_send, o_recv, gate_sem):
    half = rs_ref.shape[1]
    chunks, width, cols = cur.shape
    me, row = lax.axis_index("dom"), lax.axis_index("row")
    sib = 1 - row
    mine = pl.ds(pl.multiple_of(row * half, half), half)

    barrier = pltpu.get_barrier_semaphore()
    pl.semaphore_signal(barrier, inc=1, device_id=(me, sib), device_id_type=MESH)
    count = 1
    for l in reversed(range(levels)):
        d = 2 ** l
        for ok, peer in ((me >= d, me - d), (me + d < slices, me + d)):
            count = count + (2 if l == 0 else 1) * ok.astype(jnp.int32)

            @pl.when(ok)
            def _():
                pl.semaphore_signal(barrier, inc=1, device_id=(peer, row), device_id_type=MESH)
                if l == 0:
                    pl.semaphore_signal(barrier, inc=1, device_id=(peer, sib), device_id_type=MESH)

    def lanes_of(core, c):
        return pl.ds(pl.multiple_of(core * (chunks * cols) + c * cols, cols), cols)

    def weight(l):
        return ((lo_ref.at[0, l], lo_v.at[l, mine]), (up_ref.at[0, l], up_v.at[l, mine]))

    def own_weight(l):
        return [pltpu.make_async_copy(a, b, w_sem.at[i, l]) for i, (a, b) in enumerate(weight(l))]

    def give_weight(l):
        return [pltpu.make_async_remote_copy(a, b, w_send.at[i, l], w_recv.at[i, l], (me, sib), MESH)
                for i, (a, b) in enumerate(weight(l))]

    def own_source(c):
        return pltpu.make_async_copy(rs_ref.at[0, :, lanes_of(row, c)], cur.at[c, mine], x_sem.at[c])

    def give_source(c):
        return pltpu.make_async_remote_copy(
            rs_ref.at[0, :, lanes_of(sib, c)], cur.at[c, mine], x_send.at[c], x_recv.at[c], (me, sib), MESH)

    def sides(l):
        d = 2 ** l
        return ((me + d < slices, me + d, me >= d, low), (me >= d, me - d, me + d < slices, high))

    def send_first(c, side, peer, core, buf):
        return pltpu.make_async_remote_copy(
            first.at[core, c], buf.at[0, c, mine], f_send.at[side, core, c], f_recv.at[side, row, c], (peer, core), MESH)

    def got_first(c, side, core, buf):
        return pltpu.make_async_remote_copy(
            first.at[core, c], buf.at[0, c, pl.ds(core * half, half)], f_send.at[side, core, c], f_recv.at[side, core, c],
            (me, sib), MESH)

    def send(c, l, side, peer, buf):
        return pltpu.make_async_remote_copy(
            snd.at[l, c], buf.at[l, c], s_sem.at[side, l, c], r_sem.at[side, l, c], (peer, row), MESH)

    def keep_state(c):
        return pltpu.make_async_copy(snd.at[levels, c], state_ref.at[:, lanes_of(row, c)], l_sem.at[c])

    def give_state(c):
        return pltpu.make_async_remote_copy(
            snd.at[levels, c], state_ref.at[:, lanes_of(row, c)], o_send.at[c], o_recv.at[c], (me, sib), MESH)

    def got_state(c):
        return pltpu.make_async_remote_copy(
            snd.at[levels, c], state_ref.at[:, lanes_of(sib, c)], o_send.at[c], o_recv.at[c], (me, sib), MESH)

    def open_core(core):
        for c in range(chunks):
            for side, (to, peer, _, buf) in enumerate(sides(0)):
                @pl.when(to)
                def _():
                    send_first(c, side, peer, core, buf).start()

    def do_math(l, c):
        if c == 0:
            for copy in own_weight(l):
                copy.wait()
            for copy in give_weight(l):
                copy.wait_recv()
        if l == 0:
            own_source(c).wait()
            give_source(c).wait_recv()
        for side, (_, _, got, buf) in enumerate(sides(l)):
            weights = (lo_v, up_v)[side]

            @pl.when(got)
            def _():
                if l == 0:
                    for core in range(2):
                        got_first(c, side, core, buf).wait_recv()
                else:
                    send(c, l, side, me, buf).wait_recv()
                for at in range(0, width, BLOCK):
                    cur[c, at:at + BLOCK] += jnp.dot(
                        weights[l, at:at + BLOCK], buf[l, c], preferred_element_type=jnp.float32)

    def do_send(l, c):
        snd[l, c] = cur[c].astype(jnp.bfloat16)
        if l == levels:
            keep_state(c).start()
            give_state(c).start()
            return
        for side, (to, peer, _, buf) in enumerate(sides(l)):
            @pl.when(to)
            def _():
                send(c, l, side, peer, buf).start()

    for c in range(chunks):
        own_source(c).start()
    for l in range(levels):
        for copy in own_weight(l):
            copy.start()
    for core in range(2):
        for c in range(chunks):
            at = (core * chunks + c) * cols
            first[core, c] = rs_ref[0, :, at:at + cols].astype(jnp.bfloat16)
    pl.semaphore_wait(barrier, count)

    open_core(0)
    for c in range(chunks):
        give_source(c).start()
    for l in range(min(AHEAD, levels)):
        for copy in give_weight(l):
            copy.start()

    @pl.when(row == 1)
    def _():
        pl.semaphore_wait(gate_sem, 1)
        open_core(1)

    for l, c in schedule(chunks, levels):
        if l == levels:
            continue
        if c == 0 and l + AHEAD < levels:
            for copy in give_weight(l + AHEAD):
                copy.start()
        do_math(l, c)
        do_send(l + 1, c)
        if GATE == (l, c):
            @pl.when(row == 0)
            def _():
                pl.semaphore_signal(gate_sem, inc=1, device_id=(me, sib), device_id_type=MESH)
                open_core(1)

    for c in range(chunks):
        keep_state(c).wait()
        got_state(c).wait_recv()
    for c in range(chunks):
        give_source(c).wait_send()
        give_state(c).wait_send()
        for l in range(levels):
            for side, (to, peer, _, buf) in enumerate(sides(l)):
                @pl.when(to)
                def _():
                    if l == 0:
                        for core in range(2):
                            send_first(c, side, peer, core, buf).wait_send()
                    else:
                        send(c, l, side, peer, buf).wait_send()
    for l in range(levels):
        for copy in give_weight(l):
            copy.wait_send()


def solution(mesh):
    slices = mesh.shape["dom"]

    def body(right_side, lower_blocks, upper_blocks, final_blocks):
        _, levels, half, width = lower_blocks.shape
        rhs = right_side.shape[2]
        cols = LANES
        chunks = rhs // 2 // cols
        bf, f32 = jnp.bfloat16, jnp.float32
        any_, vm = pl.BlockSpec(memory_space=pl.ANY), pl.BlockSpec(memory_space=pltpu.VMEM)
        dma = pltpu.SemaphoreType.DMA
        state = pl.pallas_call(
            functools.partial(kernel, slices, levels),
            out_shape=jax.ShapeDtypeStruct((width, rhs), bf),
            in_specs=[vm, any_, any_],
            out_specs=vm,
            scratch_shapes=[
                pltpu.VMEM((levels, width, width), bf),
                pltpu.VMEM((levels, width, width), bf),
                pltpu.VMEM((chunks, width, cols), f32),
                pltpu.VMEM((2, chunks, half, cols), bf),
                pltpu.VMEM((levels + 1, chunks, width, cols), bf),
                pltpu.VMEM((levels, chunks, width, cols), bf),
                pltpu.VMEM((levels, chunks, width, cols), bf),
                dma((2, levels)), dma((2, levels)), dma((2, levels)),
                dma((chunks,)), dma((chunks,)), dma((chunks,)),
                dma((2, 2, chunks)), dma((2, 2, chunks)),
                dma((2, levels, chunks)), dma((2, levels, chunks)),
                dma((chunks,)), dma((chunks,)), dma((chunks,)),
                pltpu.SemaphoreType.REGULAR,
            ],
            compiler_params=pltpu.CompilerParams(
                collective_id=0, has_side_effects=True, vmem_limit_bytes=52 * 2**20),
        )(right_side, lower_blocks, upper_blocks)
        return jnp.dot(final_blocks[0], state, preferred_element_type=f32)[None]

    in_specs = (
        P("dom", "row", None),
        P("dom", None, "row", None),
        P("dom", None, "row", None),
        P("dom", "row", None),
    )
    return jax.shard_map(body, mesh=mesh, in_specs=in_specs, out_specs=P("dom", "row", None), check_vma=False)
```

time: 218 us -> 104 us (0.48); the launches traced: 215 us -> 104 us
  Pallas kernels: 0 us -> 102 us
  waiting for transfers between devices: 69.9 us -> 0 us
  starting transfers between devices: 61.4 us -> 0 us
  blocking collectives: 43 us -> 0 us
  matrix products: 29.5 us -> 0.75 us
  local copies, waits for them, and re-layouts: 8.93 us -> 1.31 us
    pallas_call x0 -> x1, Pallas kernels: none -> 102 us  [body(): pl.pallas_call(functools.partial(kernel, slices, levels), out_shape=jax.S...]
    ppermute x12 -> x0, waiting for transfers between devices: 69.9 us -> none  [shifted(): lax.ppermute(value, axis, [(source, source + steps) for source in range(f...]
    ppermute x12 -> x0, starting transfers between devices: 61.4 us -> none  [shifted(): lax.ppermute(value, axis, [(source, source + steps) for source in range(f...]
    all_to_all x7 -> x0, blocking collectives: 43 us -> none  [from_everyone(): lax.all_to_all(jnp.broadcast_to(shard[None], (count, *shard.shape)), axis...]
    dot_general x13 -> x1, matrix products: 29.5 us -> 0.75 us  [body(): return jnp.dot(final_blocks[0], state, preferred_element_type=f32)[None]]
    concatenate x6 -> x0, local copies, waits for them, and re-layouts: 4.16 us -> none  [side_by_side(): both = jnp.concatenate(arrays, axis=along)]
  transfers between devices with their start and end apart: 12 -> 0, of which waited for: 12 -> 0; matrix products, arithmetic and copies ran while one was open for 0% -> 0% of each run, Pallas kernels for 0% -> 0%
where the time goes in v2:
time: 104 us
  Pallas kernels  102 us (98%)
  local copies, waits for them, and re-layouts  1.31 us (1%)
    pallas_call x1, Pallas kernels, body(): pl.pallas_call(functools.partial(kernel, slices, levels), out_shape=jax.S...  102 us

profile of v2, /device:TPU:5, one launch (start us, length us, event | category | flops | bytes accessed | tf_op | source)
XLA Modules:
  0.0 104.0 jit_solution(14396443654833465761)
XLA Ops:
  0.0 0.0 copy-start
  0.0 101.9 %shard_map.46 = bf16[1024,512]{1,0:T(8,128)(2,1)S(1)} custom-call(f32[1,512,512]{2,1,0:T(8,128)} %rs_ref.1, bf16[1,6,512,1024]{3,2,1,0:T(8,128)(2,1)} %lo_ref.1, bf16[1,6,512,1024]{3,2,1,0:T(8,128)(2,1)} %up_ref.1), custom_call_target="tpu_custom_call" | custom-call | tf_op jit(solution)/shard_map/pallas_call | solution.py:202
  102.0 0.0 copy-done
  102.0 0.8 convolution_bitcast_fusion
  102.7 1.3 %copy.5 = f32[1,512,512]{2,1,0:T(8,128)} copy(f32[1,512,512]{1,2,0:T(8,128)S(1)} %convolution_bitcast_fusion) | data formatting | bytes 2097152 | tf_op jit(solution)/shard_map/broadcast_in_dim | solution.py:225
Async XLA Ops:
  0.0 102.0 %copy-start = (bf16[1,512,1024]{2,1,0:T(8,128)(2,1)S(1)}, bf16[1,512,1024]{2,1,0:T(8,128)(2,1)}, u32[]{:S(2)}) copy-start(bf16[1,512,1024]{2,1,0:T(8,128)(2,1)} %param.7) | copy-start | bytes 3145732

commit v3 on v2

--- a/solution.py
+++ b/solution.py
@@ -9,7 +9,7 @@
 
 MESH = pl.DeviceIdType.MESH
 LANES = 128
-BLOCK = 256
+BLOCK = 512
 AHEAD = 2
 GATE = (0, 0)
 
@@ -19,8 +19,8 @@
 
 
 def kernel(slices, levels, rs_ref, lo_ref, up_ref, state_ref,
-           lo_v, up_v, cur, first, snd, low, high,
-           w_sem, w_send, w_recv, x_sem, x_send, x_recv,
+           src_v, lo_v, up_v, cur, first, snd, low, high,
+           src_sem, w_sem, w_send, w_recv, x_sem, x_send, x_recv,
            f_send, f_recv, s_sem, r_sem, l_sem, o_send, o_recv, gate_sem):
     half = rs_ref.shape[1]
     chunks, width, cols = cur.shape
@@ -28,6 +28,8 @@
     sib = 1 - row
     mine = pl.ds(pl.multiple_of(row * half, half), half)
 
+    source = pltpu.make_async_copy(rs_ref.at[0], src_v, src_sem)
+    source.start()
     barrier = pltpu.get_barrier_semaphore()
     pl.semaphore_signal(barrier, inc=1, device_id=(me, sib), device_id_type=MESH)
     count = 1
@@ -136,10 +138,11 @@
     for l in range(levels):
         for copy in own_weight(l):
             copy.start()
+    source.wait()
     for core in range(2):
         for c in range(chunks):
             at = (core * chunks + c) * cols
-            first[core, c] = rs_ref[0, :, at:at + cols].astype(jnp.bfloat16)
+            first[core, c] = src_v[:, at:at + cols].astype(jnp.bfloat16)
     pl.semaphore_wait(barrier, count)
 
     open_core(0)
@@ -202,9 +205,10 @@
         state = pl.pallas_call(
             functools.partial(kernel, slices, levels),
             out_shape=jax.ShapeDtypeStruct((width, rhs), bf),
-            in_specs=[vm, any_, any_],
+            in_specs=[any_, any_, any_],
             out_specs=vm,
             scratch_shapes=[
+                pltpu.VMEM((half, rhs), f32),
                 pltpu.VMEM((levels, width, width), bf),
                 pltpu.VMEM((levels, width, width), bf),
                 pltpu.VMEM((chunks, width, cols), f32),
@@ -212,6 +216,7 @@
                 pltpu.VMEM((levels + 1, chunks, width, cols), bf),
                 pltpu.VMEM((levels, chunks, width, cols), bf),
                 pltpu.VMEM((levels, chunks, width, cols), bf),
+                dma,
                 dma((2, levels)), dma((2, levels)), dma((2, levels)),
                 dma((chunks,)), dma((chunks,)), dma((chunks,)),
                 dma((2, 2, chunks)), dma((2, 2, chunks)),

time: 104 us -> 103 us (level)
    pallas_call x1, Pallas kernels: 102 us -> 101 us  [body(): pl.pallas_call(functools.partial(kernel, slices, levels), out_shape=jax.S...]
where the time goes in v3:
time: 103 us
  Pallas kernels  101 us (98%)
  local copies, waits for them, and re-layouts  1.31 us (1%)
    pallas_call x1, Pallas kernels, body(): pl.pallas_call(functools.partial(kernel, slices, levels), out_shape=jax.S...  101 us

profile of v3, /device:TPU:5, one launch (start us, length us, event | category | flops | bytes accessed | tf_op | source)
XLA Modules:
  0.0 102.9 jit_solution(756258593956466657)
XLA Ops:
  0.0 0.0 copy-start
  0.0 100.8 %shard_map.46 = bf16[1024,512]{1,0:T(8,128)(2,1)S(1)} custom-call(f32[1,512,512]{2,1,0:T(8,128)} %rs_ref.1, bf16[1,6,512,1024]{3,2,1,0:T(8,128)(2,1)} %lo_ref.1, bf16[1,6,512,1024]{3,2,1,0:T(8,128)(2,1)} %up_ref.1), custom_call_target="tpu_custom_call" | custom-call | tf_op jit(solution)/shard_map/pallas_call | solution.py:205
  100.8 0.0 copy-done
  100.8 0.8 convolution_bitcast_fusion
  101.6 1.3 %copy.5 = f32[1,512,512]{2,1,0:T(8,128)} copy(f32[1,512,512]{1,2,0:T(8,128)S(1)} %convolution_bitcast_fusion) | data formatting | bytes 2097152 | tf_op jit(solution)/shard_map/broadcast_in_dim | solution.py:230
Async XLA Ops:
  0.0 100.8 %copy-start = (bf16[1,512,1024]{2,1,0:T(8,128)(2,1)S(1)}, bf16[1,512,1024]{2,1,0:T(8,128)(2,1)}, u32[]{:S(2)}) copy-start(bf16[1,512,1024]{2,1,0:T(8,128)(2,1)} %param.7) | copy-start | bytes 3145732

commit v4 on v3

--- a/solution.py
+++ b/solution.py
@@ -5,6 +5,7 @@
 from jax import lax
 from jax.experimental import pallas as pl
 from jax.experimental.pallas import tpu as pltpu
+from jax.experimental.layout import Layout, with_layout_constraint
 from jax.sharding import PartitionSpec as P
 
 MESH = pl.DeviceIdType.MESH
@@ -227,7 +228,8 @@
             compiler_params=pltpu.CompilerParams(
                 collective_id=0, has_side_effects=True, vmem_limit_bytes=52 * 2**20),
         )(right_side, lower_blocks, upper_blocks)
-        return jnp.dot(final_blocks[0], state, preferred_element_type=f32)[None]
+        product = jnp.dot(final_blocks[0], state, preferred_element_type=f32)
+        return with_layout_constraint(product, Layout(major_to_minor=(0, 1)))[None]
 
     in_specs = (
         P("dom", "row", None),

time: 103 us -> 103 us (level)
  local copies, waits for them, and re-layouts: 1.31 us -> 0.01 us
    broadcast_in_dim x1 -> x0, local copies, waits for them, and re-layouts: 1.31 us -> none  [body(): return jnp.dot(final_blocks[0], state, preferred_element_type=f32)[None]]
where the time goes in v4:
time: 103 us; the launch traced here: 102 us
  Pallas kernels  101 us (98%)
  matrix products  1.68 us (2%)
    pallas_call x1, Pallas kernels, body(): pl.pallas_call(functools.partial(kernel, slices, levels), out_shape=jax.S...  101 us

profile of v4, /device:TPU:5, one launch (start us, length us, event | category | flops | bytes accessed | tf_op | source)
XLA Modules:
  0.0 102.5 jit_solution(9369319818036117849)
XLA Ops:
  0.0 0.0 copy-start
  0.0 100.8 %shard_map.46 = bf16[1024,512]{1,0:T(8,128)(2,1)S(1)} custom-call(f32[1,512,512]{2,1,0:T(8,128)} %rs_ref.1, bf16[1,6,512,1024]{3,2,1,0:T(8,128)(2,1)} %lo_ref.1, bf16[1,6,512,1024]{3,2,1,0:T(8,128)(2,1)} %up_ref.1), custom_call_target="tpu_custom_call" | custom-call | tf_op jit(solution)/shard_map/pallas_call | solution.py:206
  100.8 0.0 copy-done
  100.8 1.7 %convolution_bitcast_fusion = f32[1,512,512]{2,1,0:T(8,128)} fusion(bf16[1024,512]{1,0:T(8,128)(2,1)S(1)} %shard_map.46, bf16[1,512,1024]{2,1,0:T(8,128)(2,1)S(1)} %copy-done), kind=kOutput, calls=%fused_computation | convolution fusion | flops 536870912 | bytes 3145728 | tf_op jit(solution)/shard_map/dot_general | solution.py:231
Async XLA Ops:
  0.0 100.8 %copy-start = (bf16[1,512,1024]{2,1,0:T(8,128)(2,1)S(1)}, bf16[1,512,1024]{2,1,0:T(8,128)(2,1)}, u32[]{:S(2)}) copy-start(bf16[1,512,1024]{2,1,0:T(8,128)(2,1)} %param.7) | copy-start | bytes 3145732

commit v5 on v4

--- a/solution.py
+++ b/solution.py
@@ -109,7 +109,7 @@
         if l == 0:
             own_source(c).wait()
             give_source(c).wait_recv()
-        for side, (_, _, got, buf) in enumerate(sides(l)):
+        for side, (_, _, got, buf) in tuple(enumerate(sides(l)))[::-1 if l in (1, 3) else 1]:
             weights = (lo_v, up_v)[side]
 
             @pl.when(got)
@@ -129,7 +129,7 @@
             keep_state(c).start()
             give_state(c).start()
             return
-        for side, (to, peer, _, buf) in enumerate(sides(l)):
+        for side, (to, peer, _, buf) in tuple(enumerate(sides(l)))[::-1 if l in (1, 3) else 1]:
             @pl.when(to)
             def _():
                 send(c, l, side, peer, buf).start()

time: 103 us -> 112 us (1.087)
  the two profiles are of different devices: /device:TPU:5 before, /device:TPU:13 now
where the time goes in v5:
time: 112 us
  Pallas kernels  110 us (98%)
  matrix products  1.68 us (2%)
    pallas_call x1, Pallas kernels, body(): pl.pallas_call(functools.partial(kernel, slices, levels), out_shape=jax.S...  110 us

profile of v5, /device:TPU:13, one launch (start us, length us, event | category | flops | bytes accessed | tf_op | source)
XLA Modules:
  0.0 112.2 jit_solution(5211289213402825733)
XLA Ops:
  0.0 0.0 copy-start
  0.0 110.5 %shard_map.46 = bf16[1024,512]{1,0:T(8,128)(2,1)S(1)} custom-call(f32[1,512,512]{2,1,0:T(8,128)} %rs_ref.1, bf16[1,6,512,1024]{3,2,1,0:T(8,128)(2,1)} %lo_ref.1, bf16[1,6,512,1024]{3,2,1,0:T(8,128)(2,1)} %up_ref.1), custom_call_target="tpu_custom_call" | custom-call | tf_op jit(solution)/shard_map/pallas_call | solution.py:206
  110.5 0.0 copy-done
  110.5 1.7 %convolution_bitcast_fusion = f32[1,512,512]{2,1,0:T(8,128)} fusion(bf16[1024,512]{1,0:T(8,128)(2,1)S(1)} %shard_map.46, bf16[1,512,1024]{2,1,0:T(8,128)(2,1)S(1)} %copy-done), kind=kOutput, calls=%fused_computation | convolution fusion | flops 536870912 | bytes 3145728 | tf_op jit(solution)/shard_map/dot_general | solution.py:231
Async XLA Ops:
  0.0 110.5 %copy-start = (bf16[1,512,1024]{2,1,0:T(8,128)(2,1)S(1)}, bf16[1,512,1024]{2,1,0:T(8,128)(2,1)}, u32[]{:S(2)}) copy-start(bf16[1,512,1024]{2,1,0:T(8,128)(2,1)} %param.7) | copy-start | bytes 3145732
